TPU v7x, 256 devices: a whole 4x4x8 slice. The times are simulated.
256 devices in a mesh: seq: 16 (over x, y), dp: 16 (over z, core).
Axes of the slice: x: 4, y: 4, z: 8, core: 2. Of those that a mesh axis runs over, the one named last changes fastest.
Arguments:
- query_rows: bfloat16 [16, 6144, 2048], P('dp', 'seq'), may hold values from -30 to 30
- key_rows: bfloat16 [16, 6144, 2048], P('dp', 'seq'), may hold values from -30 to 30
- value_rows: bfloat16 [16, 6144, 2048], P('dp', 'seq'), may hold values from -6 to 6
- key_tiles: int32 [16, 16, 4], P('dp'), may hold values from 0 to 15, as said below
- tile_counts: int32 [16, 16], P('dp'), may hold values from 2 to 4, as said below
- out_weight: bfloat16 [2048, 3072], P('dp'), may hold values from -0.125 to 0.125
- gate_vector: bfloat16 [16, 3072], P('dp'), may hold values from -4 to 4
Outputs:
- gated_out: bfloat16 [16, 6144, 3072], P('dp', 'seq')
Inputs may be any that keep to these rules, and one draw needn't show every extreme that they name: `key_tiles`: in each row of a video the 4 entries are distinct tiles of that video; only the first tile_counts entries are used. `tile_counts`: each video has some query tile that uses all 4 slots.
All inputs are finite; a program needn't handle non-finite values.
Results may differ from a plain program's by a relative error of at most 0.007.
Values may be sent and summed in bfloat16 or wider, within the bound.
A program may use at most 128 MiB of HBM per device.

v0:
```python
import math

import jax
import jax.numpy as jnp
from jax import lax
from jax.sharding import PartitionSpec as P

HD = 128
TILE = 384
MAXK = 4


def attend_local(query_heads, key_heads, value_heads, tile_list, tile_count):
    tile_total = query_heads.shape[0] // TILE
    heads_here = query_heads.shape[1] // HD
    query_tiles = query_heads.reshape(tile_total, TILE, heads_here, HD)
    key_blocks = key_heads.reshape(tile_total, TILE, heads_here, HD)
    value_blocks = value_heads.reshape(tile_total, TILE, heads_here, HD)
    score_scale = 1.0 / math.sqrt(HD)
    running_max = jnp.full((tile_total, heads_here, TILE, 1), -jnp.inf, jnp.float32)
    running_sum = jnp.zeros((tile_total, heads_here, TILE, 1), jnp.float32)
    accumulated = jnp.zeros((tile_total, TILE, heads_here, HD), jnp.float32)
    for key_slot in range(MAXK):
        chosen = tile_list[:, key_slot]
        key_chosen = jnp.take(key_blocks, chosen, axis=0)
        value_chosen = jnp.take(value_blocks, chosen, axis=0)
        scores = (
            jnp.einsum(
                "athd,ashd->ahts", query_tiles, key_chosen, preferred_element_type=jnp.float32
            )
            * score_scale
        )
        is_live = (key_slot < tile_count)[:, None, None, None]
        scores = jnp.where(is_live, scores, -jnp.inf)
        new_max = jnp.maximum(running_max, jnp.max(scores, axis=-1, keepdims=True))
        factor = jnp.exp(running_max - new_max)
        weights = jnp.exp(scores - new_max)
        running_sum = running_sum * factor + jnp.sum(weights, axis=-1, keepdims=True)
        added = jnp.einsum(
            "ahts,ashd->athd",
            weights.astype(jnp.bfloat16),
            value_chosen,
            preferred_element_type=jnp.float32,
        )
        accumulated = accumulated * jnp.transpose(factor, (0, 2, 1, 3)) + added
        running_max = new_max
    result = accumulated / jnp.transpose(running_sum, (0, 2, 1, 3))
    return result.reshape(tile_total * TILE, heads_here * HD).astype(jnp.bfloat16)


def shards(query_rows, key_rows, value_rows, key_tiles, tile_counts, out_weight, gate_vector):
    query_heads, key_heads, value_heads = (
        lax.all_to_all(query_rows[0], "seq", split_axis=1, concat_axis=0, tiled=True),
        lax.all_to_all(key_rows[0], "seq", split_axis=1, concat_axis=0, tiled=True),
        lax.all_to_all(value_rows[0], "seq", split_axis=1, concat_axis=0, tiled=True),
    )
    head_result = attend_local(query_heads, key_heads, value_heads, key_tiles[0], tile_counts[0])
    attended = lax.all_to_all(head_result, "seq", split_axis=0, concat_axis=1, tiled=True)
    projected = jnp.dot(
        attended,
        lax.all_gather(out_weight, "dp", axis=0, tiled=True),
        preferred_element_type=jnp.float32,
    )
    gated = gate_vector[0].astype(jnp.float32)[None, :] * projected
    return gated.astype(jnp.bfloat16)[None]


def solution(mesh):
    in_specs = (
        P("dp", "seq", None),
        P("dp", "seq", None),
        P("dp", "seq", None),
        P("dp", None, None),
        P("dp", None),
        P("dp", None),
        P("dp", None),
    )
    out_specs = P("dp", "seq", None)
    return jax.shard_map(shards, mesh=mesh, in_specs=in_specs, out_specs=out_specs, check_vma=False)
```

profile of v0, /device:TPU:1, one launch (start us, length us, event | category | flops | bytes accessed | tf_op | source)
XLA Modules:
  0.0 181.5 jit_solution(7563084368427351228)
XLA Ops:
  7.3 1.9 %copy.22 = bf16[1,384,2048]{1,2,0:T(8,128)(2,1)S(1)} copy(bf16[1,384,2048]{2,1,0:T(8,128)(2,1)} %param.10) | data formatting | bytes 3145728 | tf_op args[1]
  10.8 7.6 %all-to-all-start = ((bf16[384,16,128]{2,0,1:T(8,128)(2,1)}), bf16[384,16,128]{2,0,1:T(8,128)(2,1)S(1)}, u32[]{:S(2)}, u32[]{:S(2)}) async-start(bf16[384,16,128]{2,0,1:T(8,128)(2,1)} %copy.23), calls=%async_computation | async-start | bytes 3145728 | tf_op jit(solution)/shard_map/all_to_all | solution.py:54
  18.4 1.9 %copy.26 = bf16[1,384,2048]{1,2,0:T(8,128)(2,1)S(1)} copy(bf16[1,384,2048]{2,1,0:T(8,128)(2,1)} %param.11) | data formatting | bytes 3145728 | tf_op args[2]
  20.2 1.6 copy.27
  21.9 17.1 %all-to-all-done = bf16[384,16,128]{2,0,1:T(8,128)(2,1)S(1)} async-done(((bf16[384,16,128]{2,0,1:T(8,128)(2,1)}), bf16[384,16,128]{2,0,1:T(8,128)(2,1)S(1)}, u32[]{:S(2)}, u32[]{:S(2)}) %all-to-all-start) | async-done | bytes 1572896 | tf_op jit(solution)/shard_map/all_to_all | solution.py:54
  39.0 5.3 %all-to-all-start.2 = ((bf16[384,16,128]{2,0,1:T(8,128)(2,1)}), bf16[384,16,128]{2,0,1:T(8,128)(2,1)S(1)}, u32[]{:S(2)}, u32[]{:S(2)}) async-start(bf16[384,16,128]{2,0,1:T(8,128)(2,1)} %copy.27), calls=%async_computation.2 | async-start | bytes 3145728 | tf_op jit(solution)/shard_map/all_to_all | solution.py:55
  44.3 2.6 %copy.24 = bf16[1,384,2048]{1,2,0:T(8,128)(2,1)} copy(bf16[1,384,2048]{2,1,0:T(8,128)(2,1)} %param.9) | data formatting | bytes 3145728 | tf_op args[0]
  46.9 2.6 %copy.25 = bf16[384,16,128]{2,0,1:T(8,128)(2,1)} copy(bf16[384,16,128]{0,2,1:T(8,128)(2,1)} %bitcast.239) | data formatting | bytes 3145728 | tf_op jit(solution)/shard_map/all_to_all | solution.py:53
  49.5 14.8 %all-to-all-done.2 = bf16[384,16,128]{2,0,1:T(8,128)(2,1)S(1)} async-done(((bf16[384,16,128]{2,0,1:T(8,128)(2,1)}), bf16[384,16,128]{2,0,1:T(8,128)(2,1)S(1)}, u32[]{:S(2)}, u32[]{:S(2)}) %all-to-all-start.2) | async-done | bytes 1572896 | tf_op jit(solution)/shard_map/all_to_all | solution.py:55
  64.3 4.7 %all-to-all-start.1 = ((bf16[384,16,128]{2,0,1:T(8,128)(2,1)}), bf16[384,16,128]{2,0,1:T(8,128)(2,1)}, u32[]{:S(2)}, u32[]{:S(2)}) async-start(bf16[384,16,128]{2,0,1:T(8,128)(2,1)} %copy.25), calls=%async_computation.1 | async-start | bytes 3145728 | tf_op jit(solution)/shard_map/all_to_all | solution.py:53
  69.1 1.9 %gather_fusion.4 = bf16[16,384,128]{2,1,0:T(8,128)(2,1)} fusion(bf16[16,384,128]{2,1,0:T(8,128)(2,1)S(1)} %bitcast.229, s32[1024]{0:T(1024)S(1)} %pad_clamp_fusion.1), kind=kCustom, calls=%fused_computation.4.clone | custom fusion | bytes 3145792 | tf_op jit(solution)/shard_map/jit(_take)/gather | solution.py:25
  71.0 1.9 %gather_fusion.6 = bf16[16,384,128]{2,1,0:T(8,128)(2,1)} fusion(bf16[16,384,128]{2,1,0:T(8,128)(2,1)S(1)} %bitcast.230, s32[1024]{0:T(1024)S(1)} %pad_clamp_fusion), kind=kCustom, calls=%fused_computation.6.clone | custom fusion | bytes 3145792 | tf_op jit(solution)/shard_map/jit(_take)/gather | solution.py:25
  72.9 1.9 %gather_fusion.7 = bf16[16,384,128]{2,1,0:T(8,128)(2,1)} fusion(bf16[16,384,128]{2,1,0:T(8,128)(2,1)S(1)} %bitcast.233, s32[1024]{0:T(1024)S(1)} %pad_clamp_fusion), kind=kCustom, calls=%fused_computation.7.clone | custom fusion | bytes 3145792 | tf_op jit(solution)/shard_map/jit(_take)/gather | solution.py:26
  74.8 2.0 %gather_fusion.5 = bf16[16,384,128]{2,1,0:T(8,128)(2,1)} fusion(bf16[16,384,128]{2,1,0:T(8,128)(2,1)S(1)} %bitcast.234, s32[1024]{0:T(1024)S(1)} %pad_clamp_fusion.1), kind=kCustom, calls=%fused_computation.5.clone | custom fusion | bytes 3145792 | tf_op jit(solution)/shard_map/jit(_take)/gather | solution.py:26
  76.8 1.9 %gather_fusion.2 = bf16[16,384,128]{2,1,0:T(8,128)(2,1)} fusion(bf16[16,384,128]{2,1,0:T(8,128)(2,1)S(1)} %bitcast.231, s32[1024]{0:T(1024)S(1)} %pad_clamp_fusion.2), kind=kCustom, calls=%fused_computation.2.clone | custom fusion | bytes 3145792 | tf_op jit(solution)/shard_map/jit(_take)/gather | solution.py:25
  78.7 1.9 %gather_fusion.3 = bf16[16,384,128]{2,1,0:T(8,128)(2,1)} fusion(bf16[16,384,128]{2,1,0:T(8,128)(2,1)S(1)} %bitcast.235, s32[1024]{0:T(1024)S(1)} %pad_clamp_fusion.2), kind=kCustom, calls=%fused_computation.3.clone | custom fusion | bytes 3145792 | tf_op jit(solution)/shard_map/jit(_take)/gather | solution.py:26
  80.6 1.9 %gather_fusion = bf16[16,384,128]{2,1,0:T(8,128)(2,1)} fusion(bf16[16,384,128]{2,1,0:T(8,128)(2,1)S(1)} %bitcast.232, s32[1024]{0:T(1024)S(1)} %pad_clamp_fusion.3), kind=kCustom, calls=%fused_computation.clone | custom fusion | bytes 3145792 | tf_op jit(solution)/shard_map/jit(_take)/gather | solution.py:25
  82.5 2.0 %gather_fusion.1 = bf16[16,384,128]{2,1,0:T(8,128)(2,1)} fusion(bf16[16,384,128]{2,1,0:T(8,128)(2,1)S(1)} %bitcast.236, s32[1024]{0:T(1024)S(1)} %pad_clamp_fusion.3), kind=kCustom, calls=%fused_computation.1.clone | custom fusion | bytes 3145792 | tf_op jit(solution)/shard_map/jit(_take)/gather | solution.py:26
  84.4 3.7 %all-to-all-done.1 = bf16[384,16,128]{2,0,1:T(8,128)(2,1)} async-done(((bf16[384,16,128]{2,0,1:T(8,128)(2,1)}), bf16[384,16,128]{2,0,1:T(8,128)(2,1)}, u32[]{:S(2)}, u32[]{:S(2)}) %all-to-all-start.1) | async-done | bytes 1572896 | tf_op jit(solution)/shard_map/all_to_all | solution.py:53
  88.1 3.0 %bitcast_reduce_fusion.1 = (f32[16,384]{1,0:T(8,128)S(1)}, f32[16,384,384]{2,1,0:T(8,128)S(1)}) fusion(pred[16]{0:T(512)(128)(4,1)S(1)} %get-tuple-element.31, bf16[384,16,128]{2,0,1:T(8,128)(2,1)} %all-to-all-done.1, bf16[16,384,128]{2,1,0:T(8,128)(2,1)S(1)} %copy-done.6, pred[16]{0:T(512)(128)(4,1)S(1)} %get-tuple-element.24), kind=kOutput, calls=%fused_computation.12 | convolution fusion | flops 611837952 | bytes 12607520 | tf_op jit(solution)/shard_map/athd,ashd->ahts/dot_general | solution.py:28
  91.1 6.5 %bitcast_reduce_fusion = (f32[16,384]{1,0:T(8,128)S(1)}, f32[16,384,384]{2,1,0:T(8,128)}) fusion(pred[16]{0:T(512)(128)(4,1)S(1)} %get-tuple-element.30, bf16[384,16,128]{2,0,1:T(8,128)(2,1)} %all-to-all-done.1, bf16[16,384,128]{2,1,0:T(8,128)(2,1)S(1)} %copy-done.5, pred[16]{0:T(512)(128)(4,1)S(1)} %get-tuple-element.22), kind=kOutput, calls=%fused_computation.9 | convolution fusion | flops 611837952 | bytes 12607520 | tf_op jit(solution)/shard_map/athd,ashd->ahts/dot_general | solution.py:28
  97.6 3.0 %bitcast_reduce_fusion.3 = (f32[16,384]{1,0:T(8,128)S(1)}, f32[16,384,384]{2,1,0:T(8,128)S(1)}) fusion(pred[16]{0:T(512)(128)(4,1)S(1)} %get-tuple-element.29, bf16[384,16,128]{2,0,1:T(8,128)(2,1)} %all-to-all-done.1, bf16[16,384,128]{2,1,0:T(8,128)(2,1)S(1)} %copy-done.7, pred[16]{0:T(512)(128)(4,1)S(1)} %get-tuple-element.26), kind=kOutput, calls=%fused_computation.18 | convolution fusion | flops 611837952 | bytes 12607520 | tf_op jit(solution)/shard_map/athd,ashd->ahts/dot_general | solution.py:28
  100.6 2.9 %bitcast_reduce_fusion.2 = (f32[16,384]{1,0:T(8,128)S(1)}, f32[16,384,384]{2,1,0:T(8,128)S(1)}) fusion(pred[16]{0:T(512)(128)(4,1)S(1)} %get-tuple-element.28, bf16[384,16,128]{2,0,1:T(8,128)(2,1)} %all-to-all-done.1, bf16[16,384,128]{2,1,0:T(8,128)(2,1)S(1)} %copy-done.4, pred[16]{0:T(512)(128)(4,1)S(1)} %get-tuple-element.15), kind=kOutput, calls=%fused_computation.15 | convolution fusion | flops 611837952 | bytes 12607520 | tf_op jit(solution)/shard_map/athd,ashd->ahts/dot_general | solution.py:28
  103.5 4.0 %fusion.4 = (f32[16,384]{1,0:T(8,128)S(1)}, f32[16,384]{1,0:T(8,128)S(1)}) fusion(f32[16,384,384]{2,1,0:T(8,128)S(1)} %get-tuple-element.37, f32[16,384]{1,0:T(8,128)S(1)} %get-tuple-element.36, pred[16]{0:T(512)(128)(4,1)S(1)} %get-tuple-element.29, f32[16,384]{1,0:T(8,128)S(1)} %get-tuple-element.12, f32[16,384,384]{2,1,0:T(8,128)S(1)} %get-tuple-element.39, ...), kind=kLoop, calls=%fused_computation.24 | loop fusion | flops 18862080 | bytes 18972704 | tf_op jit(solution)/shard_map/reduce_sum | solution.py:38
  107.5 6.7 %fusion.8 = (f32[16,384]{1,0:T(8,128)S(1)}, f32[16,384]{1,0:T(8,128)S(1)}) fusion(f32[16,384,384]{2,1,0:T(8,128)S(1)} %get-tuple-element.35, f32[16,384]{1,0:T(8,128)S(1)} %get-tuple-element.11, pred[16]{0:T(512)(128)(4,1)S(1)} %get-tuple-element.31, f32[16,384]{1,0:T(8,128)S(1)} %get-tuple-element.10, f32[16,384,384]{2,1,0:T(8,128)} %get-tuple-element.33, ...), kind=kLoop, calls=%fused_computation.28 | loop fusion | flops 18862080 | bytes 18972704 | tf_op jit(solution)/shard_map/reduce_sum | solution.py:38
  114.2 7.9 %fusion.12 = f32[16,128,384]{2,1,0:T(8,128)} fusion(f32[16,384,384]{2,1,0:T(8,128)} %get-tuple-element.33, f32[16,384]{1,0:T(8,128)S(1)} %get-tuple-element.10, pred[16]{0:T(512)(128)(4,1)S(1)} %get-tuple-element.30, bf16[16,384,128]{2,1,0:T(8,128)(2,1)S(1)} %copy-done.3, pred[16]{0:T(512)(128)(4,1)S(1)} %get-tuple-element.22), kind=kOutput, calls=%fused_computation.32 | convolution fusion | flops 614203392 | bytes 14180384 | tf_op jit(solution)/shard_map/ahts,ashd->athd/dot_general | solution.py:39
  122.2 3.9 %fusion.14 = f32[16,128,384]{2,1,0:T(8,128)} fusion(f32[16,384,384]{2,1,0:T(8,128)S(1)} %get-tuple-element.35, f32[16,384]{1,0:T(8,128)S(1)} %get-tuple-element.11, pred[16]{0:T(512)(128)(4,1)S(1)} %get-tuple-element.31, bf16[16,384,128]{2,1,0:T(8,128)(2,1)S(1)} %copy-done.2, pred[16]{0:T(512)(128)(4,1)S(1)} %get-tuple-element.24), kind=kOutput, calls=%fused_computation.33 | convolution fusion | flops 614203392 | bytes 14180384 | tf_op jit(solution)/shard_map/ahts,ashd->athd/dot_general | solution.py:39
  126.1 3.9 %fusion.16 = f32[16,128,384]{2,1,0:T(8,128)} fusion(f32[16,384,384]{2,1,0:T(8,128)S(1)} %get-tuple-element.39, f32[16,384]{1,0:T(8,128)S(1)} %get-tuple-element.12, pred[16]{0:T(512)(128)(4,1)S(1)} %get-tuple-element.28, bf16[16,384,128]{2,1,0:T(8,128)(2,1)S(1)} %copy-done.1, pred[16]{0:T(512)(128)(4,1)S(1)} %get-tuple-element.15), kind=kOutput, calls=%fused_computation.34 | convolution fusion | flops 614203392 | bytes 14180384 | tf_op jit(solution)/shard_map/ahts,ashd->athd/dot_general | solution.py:39
  130.0 6.6 %fusion.68 = bf16[16,384,128]{1,2,0:T(8,128)(2,1)} fusion(f32[16,384]{1,0:T(8,128)S(1)} %get-tuple-element.6, f32[16,128,384]{2,1,0:T(8,128)} %fusion.12, f32[16,384]{1,0:T(8,128)S(1)} %get-tuple-element.9, f32[16,128,384]{2,1,0:T(8,128)} %fusion.14, f32[16,384]{1,0:T(8,128)S(1)} %get-tuple-element.8, f32[16,128,384]{2,1,0:T(8,128)} %fusion.16, ...), kind=kOutput, calls=%fused_computation.95 | convolution fusion | flops 621281280 | bytes 22167584 | tf_op jit(solution)/shard_map/ahts,ashd->athd/dot_general | solution.py:39
  136.6 6.9 %all-to-all-start.3 = ((bf16[16,384,128]{1,2,0:T(8,128)(2,1)}), bf16[16,384,128]{1,2,0:T(8,128)(2,1)S(1)}, u32[]{:S(2)}, u32[]{:S(2)}) async-start(bf16[16,384,128]{1,2,0:T(8,128)(2,1)} %fusion.68), calls=%async_computation.3 | async-start | bytes 3145728 | tf_op jit(solution)/shard_map/all_to_all | solution.py:58
  143.6 20.1 %all-to-all-done.3 = bf16[16,384,128]{1,2,0:T(8,128)(2,1)S(1)} async-done(((bf16[16,384,128]{1,2,0:T(8,128)(2,1)}), bf16[16,384,128]{1,2,0:T(8,128)(2,1)S(1)}, u32[]{:S(2)}, u32[]{:S(2)}) %all-to-all-start.3) | async-done | bytes 1572896 | tf_op jit(solution)/shard_map/all_to_all | solution.py:58
  163.7 11.0 %fusion.36 = bf16[1,384,3072]{2,1,0:T(8,128)(2,1)} fusion(bf16[384,2048]{0,1:T(8,128)(2,1)S(1)} %bitcast.240, bf16[2048,3072]{1,0:T(8,128)(2,1)} %all-gather.2.cloned.1.call-done, f32[3072]{0:T(1024)S(1)} %bitcast.241), kind=kOutput, calls=%fused_computation.53 | convolution fusion | flops 4834197504 | bytes 16527360 | tf_op jit(solution)/shard_map/dot_general | solution.py:59
  (35 shorter events, 2.5 us)
Async XLA Ops:
  6.5 157.2 %all-gather.2.cloned.1.call-start = ((), (), s32[]{:S(2)}) async-start(), calls=%async_computation.4 | async-start | bytes 13369344 | tf_op jit(solution)/shard_map/all_gather | solution.py:61
  10.8 28.2 %all-to-all-start = ((bf16[384,16,128]{2,0,1:T(8,128)(2,1)}), bf16[384,16,128]{2,0,1:T(8,128)(2,1)S(1)}, u32[]{:S(2)}, u32[]{:S(2)}) async-start(bf16[384,16,128]{2,0,1:T(8,128)(2,1)} %copy.23), calls=%async_computation | async-start | bytes 3145728 | tf_op jit(solution)/shard_map/all_to_all | solution.py:54
  39.0 25.4 %all-to-all-start.2 = ((bf16[384,16,128]{2,0,1:T(8,128)(2,1)}), bf16[384,16,128]{2,0,1:T(8,128)(2,1)S(1)}, u32[]{:S(2)}, u32[]{:S(2)}) async-start(bf16[384,16,128]{2,0,1:T(8,128)(2,1)} %copy.27), calls=%async_computation.2 | async-start | bytes 3145728 | tf_op jit(solution)/shard_map/all_to_all | solution.py:55
  46.9 22.1 %copy-start.9 = (s32[1,16,4]{1,2,0:T(4,128)S(1)}, s32[1,16,4]{1,2,0:T(4,128)}, u32[]{:S(2)}) copy-start(s32[1,16,4]{1,2,0:T(4,128)} %param.12) | copy-start | bytes 772
  46.9 22.2 %copy-start.10 = (s32[1,16]{1,0:T(1,128)S(1)}, s32[1,16]{1,0:T(1,128)}, u32[]{:S(2)}) copy-start(s32[1,16]{1,0:T(1,128)} %param.13) | copy-start | bytes 196
  64.3 23.8 %all-to-all-start.1 = ((bf16[384,16,128]{2,0,1:T(8,128)(2,1)}), bf16[384,16,128]{2,0,1:T(8,128)(2,1)}, u32[]{:S(2)}, u32[]{:S(2)}) async-start(bf16[384,16,128]{2,0,1:T(8,128)(2,1)} %copy.25), calls=%async_computation.1 | async-start | bytes 3145728 | tf_op jit(solution)/shard_map/all_to_all | solution.py:53
  82.5 5.6 %copy-start.6 = (bf16[16,384,128]{2,1,0:T(8,128)(2,1)S(1)}, bf16[16,384,128]{2,1,0:T(8,128)(2,1)}, u32[]{:S(2)}) copy-start(bf16[16,384,128]{2,1,0:T(8,128)(2,1)} %gather_fusion.4) | copy-start | bytes 4718596
  88.1 3.0 %copy-start.5 = (bf16[16,384,128]{2,1,0:T(8,128)(2,1)S(1)}, bf16[16,384,128]{2,1,0:T(8,128)(2,1)}, u32[]{:S(2)}) copy-start(bf16[16,384,128]{2,1,0:T(8,128)(2,1)} %gather_fusion.6) | copy-start | bytes 4718596
  91.1 6.5 %copy-start.7 = (bf16[16,384,128]{2,1,0:T(8,128)(2,1)S(1)}, bf16[16,384,128]{2,1,0:T(8,128)(2,1)}, u32[]{:S(2)}) copy-start(bf16[16,384,128]{2,1,0:T(8,128)(2,1)} %gather_fusion) | copy-start | bytes 4718596
  97.6 3.0 %copy-start.4 = (bf16[16,384,128]{2,1,0:T(8,128)(2,1)S(1)}, bf16[16,384,128]{2,1,0:T(8,128)(2,1)}, u32[]{:S(2)}) copy-start(bf16[16,384,128]{2,1,0:T(8,128)(2,1)} %gather_fusion.2) | copy-start | bytes 4718596
  107.5 6.7 %copy-start.3 = (bf16[16,384,128]{2,1,0:T(8,128)(2,1)S(1)}, bf16[16,384,128]{2,1,0:T(8,128)(2,1)}, u32[]{:S(2)}) copy-start(bf16[16,384,128]{2,1,0:T(8,128)(2,1)} %gather_fusion.7) | copy-start | bytes 4718596
  114.2 8.0 %copy-start.2 = (bf16[16,384,128]{2,1,0:T(8,128)(2,1)S(1)}, bf16[16,384,128]{2,1,0:T(8,128)(2,1)}, u32[]{:S(2)}) copy-start(bf16[16,384,128]{2,1,0:T(8,128)(2,1)} %gather_fusion.5) | copy-start | bytes 4718596
  122.2 3.9 %copy-start.1 = (bf16[16,384,128]{2,1,0:T(8,128)(2,1)S(1)}, bf16[16,384,128]{2,1,0:T(8,128)(2,1)}, u32[]{:S(2)}) copy-start(bf16[16,384,128]{2,1,0:T(8,128)(2,1)} %gather_fusion.3) | copy-start | bytes 4718596
  126.1 3.9 %copy-start = (bf16[16,384,128]{2,1,0:T(8,128)(2,1)S(1)}, bf16[16,384,128]{2,1,0:T(8,128)(2,1)}, u32[]{:S(2)}) copy-start(bf16[16,384,128]{2,1,0:T(8,128)(2,1)} %gather_fusion.1) | copy-start | bytes 4718596
  136.6 6.9 %copy-start.8 = (bf16[1,3072]{1,0:T(2,128)(2,1)S(1)}, bf16[1,3072]{1,0:T(2,128)(2,1)}, u32[]{:S(2)}) copy-start(bf16[1,3072]{1,0:T(2,128)(2,1)} %param.15) | copy-start | bytes 18436
  136.6 27.1 %all-to-all-start.3 = ((bf16[16,384,128]{1,2,0:T(8,128)(2,1)}), bf16[16,384,128]{1,2,0:T(8,128)(2,1)S(1)}, u32[]{:S(2)}, u32[]{:S(2)}) async-start(bf16[16,384,128]{1,2,0:T(8,128)(2,1)} %fusion.68), calls=%async_computation.3 | async-start | bytes 3145728 | tf_op jit(solution)/shard_map/all_to_all | solution.py:58
Sparse Core Ops, SparseCore 0:
  9.2 79.8 all-gather.1
where the time goes:
time: 185 us; the launch traced here: 182 us
  waiting for transfers between devices  56.4 us (30%)
  matrix products  48.7 us (26%)
  local copies, waits for them, and re-layouts  27.6 us (15%)
  starting transfers between devices  24.5 us (13%)
  between operations  13.6 us (7%)
  other arithmetic  10.8 us (6%)
    dot_general x4, matrix products, attend_local(): jnp.einsum('ahts,ashd->athd', weights.astype(jnp.bfloat16), value_chosen,...  22.4 us
    all_to_all x1, waiting for transfers between devices, shards(): lax.all_to_all(head_result, 'seq', split_axis=0, concat_axis=1, tiled=True)  20.1 us
    all_to_all x1, waiting for transfers between devices, shards(): lax.all_to_all(key_rows[0], 'seq', split_axis=1, concat_axis=0, tiled=True)  17.1 us
    dot_general x4, matrix products, attend_local(): jnp.einsum('athd,ashd->ahts', query_tiles, key_chosen, preferred_element_...  15.3 us
    all_to_all x1, waiting for transfers between devices, shards(): lax.all_to_all(value_rows[0], 'seq', split_axis=1, concat_axis=0, tiled=T...  14.8 us
    dot_general x1, matrix products, shards(): jnp.dot(attended, lax.all_gather(out_weight, 'dp', axis=0, tiled=True), p...  11 us
    reduce_sum x2, other arithmetic, attend_local(): jnp.sum(weights, axis=-1, keepdims=True)  10.7 us
    gather x4, local copies, waits for them, and re-layouts, attend_local(): value_chosen = jnp.take(value_blocks, chosen, axis=0)  7.72 us
  transfers between devices with their start and end apart: 5, of which 4 were waited for; matrix products, arithmetic and copies ran while one was open for 42% of the time, Pallas kernels for 0%

commit v1 on v0

v1 whole, which is shorter than its diff:
```python
import math

import jax
import jax.numpy as jnp
from jax import lax
from jax.experimental import pallas as pl
from jax.experimental.pallas import tpu as pltpu
from jax.sharding import PartitionSpec as P

HD = 128
TILE = 384
MAXK = 4
SIDE = 4
RING = 8
PEERS = SIDE * SIDE - 1
D = 3072
SUBS = 2
PIECE = HD // (2 * SUBS)
NCHUNK = 512
MESH = pl.DeviceIdType.MESH
ORDER_X = (1, 3, 0, 0, 1, 3, 1, 3, 2, 2, 1, 3, 2, 2, 0, 0)
ORDER_Y = (0, 0, 1, 3, 1, 3, 3, 1, 1, 3, 2, 2, 2, 0, 2, 0)
TO_EXP2 = math.log2(math.e) / math.sqrt(HD)


def packed(digits):
    value = sum(d << (2 * i) for i, d in enumerate(digits))
    return value - (1 << 32) if value >= 1 << 31 else value


def digit(digits, i):
    if isinstance(i, int):
        return digits[i]
    return lax.shift_right_logical(jnp.int32(packed(digits)), 2 * i) & 3


def attend(query, kbuf, vbuf, key_tiles, tile_counts, a):
    count = tile_counts[a]
    scores, tops, biases = [], [], []
    for j in range(MAXK):
        s = lax.dot_general(
            query, kbuf[key_tiles[a, j]], (((1,), (1,)), ((), ())), preferred_element_type=jnp.float32
        )
        bias = jnp.where(j < count, 0.0, -jnp.inf).astype(jnp.float32)
        top = jnp.maximum(jnp.maximum(s[:, :HD], s[:, HD : 2 * HD]), s[:, 2 * HD :])
        scores.append(s)
        biases.append(bias)
        tops.append(top if j < 2 else top + bias)
    top = jnp.maximum(jnp.maximum(tops[0], tops[1]), jnp.maximum(tops[2], tops[3]))
    row_top = jnp.max(top, axis=-1, keepdims=True)
    parts, mixed = [], None
    for j in range(MAXK):
        shift = row_top if j < 2 else row_top - biases[j]
        weights = jnp.exp2((scores[j] - shift) * TO_EXP2)
        parts.append(weights[:, :HD] + weights[:, HD : 2 * HD] + weights[:, 2 * HD :])
        part = jnp.dot(
            weights.astype(jnp.bfloat16), vbuf[key_tiles[a, j]], preferred_element_type=jnp.float32
        )
        mixed = part if mixed is None else mixed + part
    total = jnp.sum((parts[0] + parts[1]) + (parts[2] + parts[3]), axis=-1, keepdims=True)
    return (mixed / total).astype(jnp.bfloat16)


def kernel(
    query_rows, key_rows, value_rows, key_tiles, tile_counts, weight, gate, out,
    kbuf, vbuf, qbuf, obuf, orecv, wbuf, acc,
    k_send, k_recv, v_send, v_recv, q_send, q_recv, o_send, o_recv, own_sem,
    w_send, w_recv, c_send, c_recv,
):
    seq, dp = lax.axis_index("seq"), lax.axis_index("dp")
    x, y, z, core = seq // SIDE, seq % SIDE, dp // 2, dp % 2
    other = z * 2 + 1 - core
    nexts = (((z + 1) % RING) * 2 + core, ((z + RING - 1) % RING) * 2 + core)

    def partner(i, sign=1):
        dx, dy = digit(ORDER_X, i), digit(ORDER_Y, i)
        return ((x + sign * dx + SIDE) % SIDE) * SIDE + (y + sign * dy + SIDE) % SIDE

    def remote(src, dst, send, recv, where):
        return pltpu.make_async_remote_copy(
            src_ref=src, dst_ref=dst, send_sem=send, recv_sem=recv, device_id=where, device_id_type=MESH
        )

    barrier = pltpu.get_barrier_semaphore()
    for i in range(PEERS):
        pl.semaphore_signal(barrier, inc=1, device_id=(partner(i), dp), device_id_type=MESH)
    for where in (*nexts, other):
        pl.semaphore_signal(barrier, inc=1, device_id=(seq, where), device_id_type=MESH)

    def head_columns(i):
        return pl.ds(pl.multiple_of(partner(i) * HD, HD), HD)

    mine = pl.ds(pl.multiple_of(seq * HD, HD), HD)
    own = [
        pltpu.make_async_copy(key_rows.at[:, mine], kbuf.at[seq], own_sem.at[0]),
        pltpu.make_async_copy(value_rows.at[:, mine], vbuf.at[seq], own_sem.at[1]),
        pltpu.make_async_copy(query_rows.at[:, mine], qbuf.at[PEERS], own_sem.at[2]),
        pltpu.make_async_copy(weight, wbuf.at[dp], own_sem.at[3]),
    ]
    for copy in own:
        copy.start()
    pl.semaphore_wait(barrier, PEERS + 3)

    def piece(p):
        return pl.ds(p * PIECE, PIECE)

    def hop(p, t, block, src=None):
        place = wbuf.at[block, piece(p)]
        return remote(place if src is None else src, place, w_send.at[p, t], w_recv.at[p, t], (seq, nexts[p // SUBS]))

    def swap(p, t, block, src=None):
        place = wbuf.at[block, piece(p)]
        return remote(place if src is None else src, place, c_send.at[p, t], c_recv.at[p, t], (seq, other))

    def block_of(p, t, which):
        return ((z - t + RING) % RING if p < SUBS else (z + t) % RING) * 2 + which

    for p in range(2 * SUBS):
        hop(p, 0, dp, weight.at[piece(p)]).start()

    for i in range(PEERS):
        remote(key_rows.at[:, head_columns(i)], kbuf.at[seq], k_send, k_recv, (partner(i), dp)).start()
    for i in range(PEERS):
        remote(value_rows.at[:, head_columns(i)], vbuf.at[seq], v_send, v_recv, (partner(i), dp)).start()
    for i in range(PEERS):
        remote(query_rows.at[:, head_columns(i)], qbuf.at[i], q_send, q_recv.at[i], (partner(i), dp)).start()
    for p in range(2 * SUBS):
        swap(p, 0, dp, weight.at[piece(p)]).start()

    def tick(t, sub):
        for p in (sub, SUBS + sub):
            block = block_of(p, t, core)
            hop(p, t - 1, block).wait_recv()

            @pl.when(t < RING - 1)
            def _():
                hop(p, t, block).start()

            swap(p, t, block).start()

    for t in (1, 2, 3):
        for sub in range(SUBS):
            tick(t, sub)
    all_but_one = pl.ds(0, PEERS)
    for copy in own:
        copy.wait()
    pltpu.make_async_copy(kbuf.at[all_but_one], kbuf.at[all_but_one], k_recv).wait()
    pltpu.make_async_copy(vbuf.at[all_but_one], vbuf.at[all_but_one], v_recv).wait()

    orecv[PEERS] = attend(qbuf[PEERS], kbuf, vbuf, key_tiles, tile_counts, seq)

    def answer(i):
        a = partner(i, -1)
        return remote(obuf.at[i], orecv.at[i], o_send.at[i], o_recv.at[i], (a, dp))

    def step(i, carry):
        a = partner(i, -1)

        @pl.when(i % 2 == 0)
        def _():
            u = i // 2
            for sub in range(SUBS):

                @pl.when(u % 2 == sub)
                def _():
                    tick(4 + u // 2, sub)

        pltpu.make_async_copy(qbuf.at[i], qbuf.at[i], q_recv.at[i]).wait()
        obuf[i] = attend(qbuf[i], kbuf, vbuf, key_tiles, tile_counts, a)
        answer(i).start()
        return carry

    lax.fori_loop(0, PEERS, step, 0)

    for p in range(2 * SUBS):
        for t in range(RING):
            swap(p, t, block_of(p, t, 1 - core)).wait_recv()

    group = 4
    for g in range(0, PEERS + 1, group):
        for i in range(g, min(g + group, PEERS)):
            pltpu.make_async_copy(orecv.at[i], orecv.at[i], o_recv.at[i]).wait()
        rows = jnp.concatenate([orecv[i] for i in range(g, g + group)], axis=1)

        def project(n, carry):
            at = pl.ds(pl.multiple_of(n * NCHUNK, NCHUNK), NCHUNK)
            block = jnp.concatenate([wbuf[partner(i), :, at] for i in range(g, g + group)], axis=0)
            product = jnp.dot(rows, block, preferred_element_type=jnp.float32)
            if g > 0:
                product = acc[:, at] + product
            if g + group <= PEERS:
                acc[:, at] = product
            else:
                out[:, at] = (gate[:, at].astype(jnp.float32) * product).astype(jnp.bfloat16)
            return carry

        lax.fori_loop(0, D // NCHUNK, project, 0)

    pltpu.make_async_copy(kbuf.at[all_but_one], kbuf.at[all_but_one], k_send).wait()
    pltpu.make_async_copy(vbuf.at[all_but_one], vbuf.at[all_but_one], v_send).wait()
    pltpu.make_async_copy(qbuf.at[all_but_one], qbuf.at[all_but_one], q_send).wait()
    for i in range(PEERS):
        answer(i).wait_send()
    for p in range(2 * SUBS):
        for t in range(RING):
            swap(p, t, dp).wait_send()
            if t < RING - 1:
                hop(p, t, dp).wait_send()


def shards(query_rows, key_rows, value_rows, key_tiles, tile_counts, out_weight, gate_vector):
    dma = pltpu.SemaphoreType.DMA
    far = pl.BlockSpec(memory_space=pltpu.HBM)
    near = pl.BlockSpec(memory_space=pltpu.VMEM)
    scalars = pl.BlockSpec(memory_space=pltpu.SMEM)
    tiles = PEERS + 1
    blocks = RING * 2
    result = pl.pallas_call(
        kernel,
        name="attention_and_projection",
        out_shape=jax.ShapeDtypeStruct((TILE, D), jnp.bfloat16),
        in_specs=[far, far, far, scalars, scalars, far, near],
        out_specs=near,
        scratch_shapes=[
            pltpu.VMEM((tiles, TILE, HD), jnp.bfloat16),
            pltpu.VMEM((tiles, TILE, HD), jnp.bfloat16),
            pltpu.VMEM((tiles, TILE, HD), jnp.bfloat16),
            pltpu.VMEM((tiles, TILE, HD), jnp.bfloat16),
            pltpu.VMEM((tiles, TILE, HD), jnp.bfloat16),
            pltpu.VMEM((blocks, HD, D), jnp.bfloat16),
            pltpu.VMEM((TILE, D), jnp.float32),
            dma, dma, dma, dma, dma, dma((tiles,)), dma((tiles,)), dma((tiles,)), dma((4,)),
            dma((2 * SUBS, RING)), dma((2 * SUBS, RING)), dma((2 * SUBS, RING)), dma((2 * SUBS, RING)),
        ],
        compiler_params=pltpu.CompilerParams(
            collective_id=0, has_side_effects=True, vmem_limit_bytes=60 << 20
        ),
        cost_estimate=pl.CostEstimate(
            flops=10_000_000_000, bytes_accessed=10_000_000, transcendentals=9_000_000
        ),
    )(query_rows[0], key_rows[0], value_rows[0], key_tiles[0], tile_counts[0], out_weight, gate_vector)
    return result[None]


def solution(mesh):
    in_specs = (
        P("dp", "seq", None),
        P("dp", "seq", None),
        P("dp", "seq", None),
        P("dp", None, None),
        P("dp", None),
        P("dp", None),
        P("dp", None),
    )
    out_specs = P("dp", "seq", None)
    return jax.shard_map(shards, mesh=mesh, in_specs=in_specs, out_specs=out_specs, check_vma=False)
```

time: 185 us -> 95.9 us (0.52); the launches traced: 182 us -> 95.7 us
  Pallas kernels: 0 us -> 91.1 us
  waiting for transfers between devices: 56.4 us -> 0 us
  matrix products: 48.7 us -> 0 us
  starting transfers between devices: 24.5 us -> 0 us
  local copies, waits for them, and re-layouts: 27.6 us -> 4.58 us
  between operations: 13.6 us -> 0.01 us
  other arithmetic: 10.8 us -> 0 us
    pallas_call x0 -> x1, Pallas kernels: none -> 91.1 us  [shards(): pl.pallas_call(kernel, name='attention_and_projection', out_shape=jax.Sha...]
    all_to_all x4 -> x0, waiting for transfers between devices: 55.7 us -> none  [the longest x1 20.1 us: shards(): lax.all_to_all(head_result, 'seq', split_axis=0, concat_axis=1, tiled=True)]
    dot_general x9 -> x0, matrix products: 48.7 us -> none  [the longest x4 22.4 us: attend_local(): jnp.einsum('ahts,ashd->athd', weights.astype(jnp.bfloat16), value_chosen,...]
    all_to_all x4 -> x0, starting transfers between devices: 24.5 us -> none  [the longest x1 7.58 us: shards(): lax.all_to_all(key_rows[0], 'seq', split_axis=1, concat_axis=0, tiled=True)]
    gather x8 -> x0, local copies, waits for them, and re-layouts: 15.3 us -> none  [the longest x4 7.72 us: attend_local(): value_chosen = jnp.take(value_blocks, chosen, axis=0)]
    reduce_sum x2 -> x0, other arithmetic: 10.7 us -> none  [attend_local(): jnp.sum(weights, axis=-1, keepdims=True)]
    all_to_all x3 -> x0, local copies, waits for them, and re-layouts: 5.9 us -> none  [the longest x1 2.63 us: shards(): lax.all_to_all(query_rows[0], 'seq', split_axis=1, concat_axis=0, tiled=T...]
    unnamed x25 -> x1, local copies, waits for them, and re-layouts: 6.37 us -> 3.22 us
  transfers between devices with their start and end apart: 5 -> 0, of which waited for: 4 -> 0; matrix products, arithmetic and copies ran while one was open for 42% -> 0% of each run, Pallas kernels for 0% -> 0%
where the time goes in v1:
time: 95.9 us; the launch traced here: 95.7 us
  Pallas kernels  91.1 us (95%)
  local copies, waits for them, and re-layouts  4.58 us (5%)
    pallas_call x1, Pallas kernels, shards(): pl.pallas_call(kernel, name='attention_and_projection', out_shape=jax.Sha...  91.1 us
    unnamed x1, local copies, waits for them, and re-layouts  3.22 us

profile of v1, /device:TPU:1, one launch (start us, length us, event | category | flops | bytes accessed | tf_op | source)
XLA Modules:
  0.0 95.7 jit_solution(3412388817278981577)
XLA Ops:
  0.0 1.4 %copy.8.key_tiles = s32[16,4]{1,0:T(8,128)} copy(s32[16,4]{0,1:T(4,128)} %bitcast.7) | data formatting | bytes 512 | tf_op jit(solution)/shard_map/squeeze | solution.py:241
  1.4 91.1 %attention_and_projection.1 = bf16[384,3072]{1,0:T(8,128)(2,1)} custom-call(bf16[384,2048]{1,0:T(8,128)(2,1)} %bitcast.8, bf16[384,2048]{1,0:T(8,128)(2,1)} %bitcast.9, bf16[384,2048]{1,0:T(8,128)(2,1)} %bitcast.10, s32[16,4]{1,0:T(8,128)} %copy.8.key_tiles, s32[16]{0:T(128)} %bitcast.11, bf16[128,3072]{1,0:T(8,128)(2,1)} %weight.1, bf16[1,3072]{1,0:T(2,128)(2,1)} %gate.1), custom_call_target="tpu_custom_call" | custom-call | flops 10000000000 | bytes 10000000 | tf_op jit(solution)/shard_map/attention_and_projection/pallas_call | solution.py:218
  92.5 3.2 %copy.10 = bf16[1,384,3072]{2,1,0:T(8,128)(2,1)} copy(bf16[1,384,3072]{2,1,0:T(8,128)(2,1)} %bitcast.6) | data formatting | bytes 4718592

commit v2 on v1

v2 whole, which is shorter than its diff:
```python
import math

import jax
import jax.numpy as jnp
from jax import lax
from jax.experimental import pallas as pl
from jax.experimental.pallas import tpu as pltpu
from jax.sharding import PartitionSpec as P

HD = 128
TILE = 384
MAXK = 4
SIDE = 4
RING = 8
PEERS = SIDE * SIDE - 1
D = 3072
PIECES = 4
PIECE = HD // PIECES
AWAY = RING // 2 - 1
COMING = AWAY * PIECES + PIECES // 2
EARLY = 7
NCHUNK = 512
LAST = 2
MESH = pl.DeviceIdType.MESH
ORDER_X = (1, 3, 0, 0, 1, 3, 1, 3, 2, 2, 1, 3, 2, 2, 0, 0)
ORDER_Y = (0, 0, 1, 3, 1, 3, 3, 1, 1, 3, 2, 2, 2, 0, 2, 0)
TO_EXP2 = math.log2(math.e) / math.sqrt(HD)


def packed(digits):
    value = sum(d << (2 * i) for i, d in enumerate(digits))
    return value - (1 << 32) if value >= 1 << 31 else value


def digit(digits, i):
    if isinstance(i, int):
        return digits[i]
    return lax.shift_right_logical(jnp.int32(packed(digits)), 2 * i) & 3


def turn(n):
    if isinstance(n, int):
        return LAST if n == PEERS - 1 else n + (n >= LAST)
    return jnp.where(n == PEERS - 1, LAST, jnp.where(n < LAST, n, n + 1))


def attend(query, kbuf, vbuf, key_tiles, tile_counts, a):
    count = tile_counts[a]
    scores, tops, biases = [], [], []
    for j in range(MAXK):
        s = lax.dot_general(
            query, kbuf[key_tiles[j, a]], (((1,), (1,)), ((), ())), preferred_element_type=jnp.float32
        )
        bias = jnp.where(j < count, 0.0, -jnp.inf).astype(jnp.float32)
        top = jnp.maximum(jnp.maximum(s[:, :HD], s[:, HD : 2 * HD]), s[:, 2 * HD :])
        scores.append(s)
        biases.append(bias)
        tops.append(top if j < 2 else top + bias)
    top = jnp.maximum(jnp.maximum(tops[0], tops[1]), jnp.maximum(tops[2], tops[3]))
    row_top = jnp.max(top, axis=-1, keepdims=True)
    parts, mixed = [], None
    for j in range(MAXK):
        shift = row_top if j < 2 else row_top - biases[j]
        weights = jnp.exp2((scores[j] - shift) * TO_EXP2)
        parts.append(weights[:, :HD] + weights[:, HD : 2 * HD] + weights[:, 2 * HD :])
        part = jnp.dot(
            weights.astype(jnp.bfloat16), vbuf[key_tiles[j, a]], preferred_element_type=jnp.float32
        )
        mixed = part if mixed is None else mixed + part
    total = jnp.sum((parts[0] + parts[1]) + (parts[2] + parts[3]), axis=-1, keepdims=True)
    return (mixed / total).astype(jnp.bfloat16)


def kernel(
    query_rows, key_rows, value_rows, key_tiles, tile_counts, weight, gate, out,
    kbuf, vbuf, qbuf, obuf, orecv, wbuf, acc,
    k_send, k_recv, v_send, v_recv, q_send, q_recv, o_send, o_recv, own_sem,
    w_send, w_recv, c_send, c_recv,
):
    seq, dp = lax.axis_index("seq"), lax.axis_index("dp")
    x, y, z, core = seq // SIDE, seq % SIDE, dp // 2, dp % 2
    other = z * 2 + 1 - core
    nexts = (((z + 1) % RING) * 2 + core, ((z + RING - 1) % RING) * 2 + core)

    def partner(i, sign=1):
        dx, dy = digit(ORDER_X, i), digit(ORDER_Y, i)
        return ((x + sign * dx + SIDE) % SIDE) * SIDE + (y + sign * dy + SIDE) % SIDE

    def remote(src, dst, send, recv, where):
        return pltpu.make_async_remote_copy(
            src_ref=src, dst_ref=dst, send_sem=send, recv_sem=recv, device_id=where, device_id_type=MESH
        )

    def bytes_of(buffer, count, semaphore):
        part = buffer.at[pl.ds(0, count)]
        return pltpu.make_async_copy(part, part, semaphore)

    barrier = pltpu.get_barrier_semaphore()
    for i in range(PEERS):
        pl.semaphore_signal(barrier, inc=1, device_id=(partner(i), dp), device_id_type=MESH)
    for where in (*nexts, other):
        pl.semaphore_signal(barrier, inc=1, device_id=(seq, where), device_id_type=MESH)

    def head_columns(i):
        return pl.ds(pl.multiple_of(partner(i) * HD, HD), HD)

    mine = pl.ds(pl.multiple_of(seq * HD, HD), HD)
    own = [
        pltpu.make_async_copy(key_rows.at[:, mine], kbuf.at[seq], own_sem),
        pltpu.make_async_copy(value_rows.at[:, mine], vbuf.at[seq], own_sem),
        pltpu.make_async_copy(query_rows.at[:, mine], qbuf.at[PEERS], own_sem),
        pltpu.make_async_copy(weight, wbuf.at[dp], own_sem),
    ]
    for copy in own:
        copy.start()
    pl.semaphore_wait(barrier, PEERS + 3)

    def piece(p):
        return pl.ds(pl.multiple_of(p * PIECE, PIECE), PIECE)

    def hop(way, n, p, block, src=None):
        place = wbuf.at[block, piece(p)]
        return remote(place if src is None else src, place, w_send, w_recv.at[way, n], (seq, nexts[way]))

    for p in range(PIECES):
        for way in range(2):
            hop(way, p, p, dp, weight.at[piece(p)]).start()

    for i in range(PEERS):
        remote(key_rows.at[:, head_columns(i)], kbuf.at[seq], k_send, k_recv, (partner(i), dp)).start()
    for i in range(PEERS):
        remote(value_rows.at[:, head_columns(i)], vbuf.at[seq], v_send, v_recv, (partner(i), dp)).start()
    for i in range(PEERS):
        remote(query_rows.at[:, head_columns(i)], qbuf.at[i], q_send, q_recv.at[i], (partner(i), dp)).start()
    remote(weight, wbuf.at[dp], c_send, c_recv, (seq, other)).start()

    def tick(n):
        q = n % PIECES
        for way in range(2):
            p = q + way * (PIECES // 2) * (n // (AWAY * PIECES))
            far = n // PIECES + 1
            block = ((z + RING - far) % RING if way == 0 else (z + far) % RING) * 2 + core
            hop(way, n, p, block).wait_recv()

            @pl.when((n < (AWAY - 1) * PIECES) | ((n < AWAY * PIECES) & (q // (PIECES // 2) == way)))
            def _():
                last = AWAY * PIECES + q % (PIECES // 2)
                hop(way, jnp.where(n < (AWAY - 1) * PIECES, n + PIECES, last), p, block).start()

            place = wbuf.at[block, piece(p)]
            remote(place, place, c_send, c_recv, (seq, other)).start()

    for n in range(EARLY):
        tick(n)
    bytes_of(kbuf, len(own) - 1 + HD * D // (TILE * HD), own_sem).wait()
    bytes_of(kbuf, PEERS, k_recv).wait()
    bytes_of(vbuf, PEERS, v_recv).wait()

    orecv[PEERS] = attend(qbuf[PEERS], kbuf, vbuf, key_tiles, tile_counts, seq)

    def answer(i):
        a = partner(i, -1)
        return remote(obuf.at[i], orecv.at[i], o_send, o_recv.at[i], (a, dp))

    def step(n, carry):
        i = turn(n)
        a = partner(i, -1)

        @pl.when(n % 3 == 1)
        def _():
            tick(EARLY + n // 3)

        pltpu.make_async_copy(qbuf.at[i], qbuf.at[i], q_recv.at[i]).wait()
        obuf[i] = attend(qbuf[i], kbuf, vbuf, key_tiles, tile_counts, a)
        answer(i).start()
        return carry

    lax.fori_loop(0, PEERS, step, 0)
    for n in range(EARLY + PEERS // 3, COMING):
        tick(n)
    bytes_of(wbuf, RING, c_recv).wait()

    order = [PEERS, *(turn(n) for n in range(PEERS))]
    done = 0
    for group in (4, 4, 4, 2, 2):
        these = order[done : done + group]
        done += group
        for i in these:
            if i < PEERS:
                pltpu.make_async_copy(orecv.at[i], orecv.at[i], o_recv.at[i]).wait()
        rows = jnp.concatenate([orecv[i] for i in these], axis=1)
        for n in range(0, D, NCHUNK):
            at = pl.ds(n, NCHUNK)
            block = jnp.concatenate([wbuf[partner(i), :, at] for i in these], axis=0)
            product = jnp.dot(rows, block, preferred_element_type=jnp.float32)
            if done > group:
                product = acc[:, at] + product
            if done <= PEERS:
                acc[:, at] = product
            else:
                out[:, at] = (gate[:, at].astype(jnp.float32) * product).astype(jnp.bfloat16)

    bytes_of(kbuf, PEERS, k_send).wait()
    bytes_of(vbuf, PEERS, v_send).wait()
    bytes_of(qbuf, PEERS, q_send).wait()
    bytes_of(obuf, PEERS, o_send).wait()
    bytes_of(wbuf, RING - 1, w_send).wait()
    bytes_of(wbuf, RING, c_send).wait()


def shards(query_rows, key_rows, value_rows, key_tiles, tile_counts, out_weight, gate_vector):
    dma = pltpu.SemaphoreType.DMA
    far = pl.BlockSpec(memory_space=pltpu.HBM)
    near = pl.BlockSpec(memory_space=pltpu.VMEM)
    scalars = pl.BlockSpec(memory_space=pltpu.SMEM)
    tiles = PEERS + 1
    blocks = RING * 2
    result = pl.pallas_call(
        kernel,
        name="attention_and_projection",
        out_shape=pltpu.VMEM((TILE, D), jnp.bfloat16),
        in_specs=[far, far, far, scalars, scalars, far, near],
        out_specs=near,
        scratch_shapes=[
            pltpu.VMEM((tiles, TILE, HD), jnp.bfloat16),
            pltpu.VMEM((tiles, TILE, HD), jnp.bfloat16),
            pltpu.VMEM((tiles, TILE, HD), jnp.bfloat16),
            pltpu.VMEM((tiles, TILE, HD), jnp.bfloat16),
            pltpu.VMEM((tiles, TILE, HD), jnp.bfloat16),
            pltpu.VMEM((blocks, HD, D), jnp.bfloat16),
            pltpu.VMEM((TILE, D), jnp.float32),
            dma, dma, dma, dma, dma, dma((PEERS,)), dma, dma((PEERS,)), dma,
            dma, dma((2, COMING)), dma, dma,
        ],
        compiler_params=pltpu.CompilerParams(
            collective_id=0, has_side_effects=True, vmem_limit_bytes=60 << 20
        ),
        cost_estimate=pl.CostEstimate(
            flops=10_000_000_000, bytes_accessed=10_000_000, transcendentals=9_000_000
        ),
    )(query_rows[0], key_rows[0], value_rows[0], key_tiles[0].T, tile_counts[0], out_weight, gate_vector)
    return result[None]


def solution(mesh):
    in_specs = (
        P("dp", "seq", None),
        P("dp", "seq", None),
        P("dp", "seq", None),
        P("dp", None, None),
        P("dp", None),
        P("dp", None),
        P("dp", None),
    )
    out_specs = P("dp", "seq", None)
    return jax.shard_map(shards, mesh=mesh, in_specs=in_specs, out_specs=out_specs, check_vma=False)
```

time: 95.9 us -> 83.5 us (0.87)
  Pallas kernels: 91.1 us -> 82 us
  local copies, waits for them, and re-layouts: 4.58 us -> 1.41 us
    pallas_call x1, Pallas kernels: 91.1 us -> 82 us  [shards(): pl.pallas_call(kernel, name='attention_and_projection', out_shape=pltpu.V...]
    unnamed x1, local copies, waits for them, and re-layouts: 3.22 us -> 1.41 us
    squeeze x1 -> x0, local copies, waits for them, and re-layouts: 1.35 us -> none  [shards(): key_tiles[0]]
where the time goes in v2:
time: 83.5 us; the launch traced here: 83.4 us
  Pallas kernels  82 us (98%)
  local copies, waits for them, and re-layouts  1.41 us (2%)
    pallas_call x1, Pallas kernels, shards(): pl.pallas_call(kernel, name='attention_and_projection', out_shape=pltpu.V...  82 us

profile of v2, /device:TPU:1, one launch (start us, length us, event | category | flops | bytes accessed | tf_op | source)
XLA Modules:
  0.0 83.4 jit_solution(15840793755012200347)
XLA Ops:
  0.0 82.0 %attention_and_projection.1 = bf16[384,3072]{1,0:T(8,128)(2,1)S(1)} custom-call(bf16[384,2048]{1,0:T(8,128)(2,1)} %bitcast.9, bf16[384,2048]{1,0:T(8,128)(2,1)} %bitcast.10, bf16[384,2048]{1,0:T(8,128)(2,1)} %bitcast.11, s32[4,16]{1,0:T(4,128)} %bitcast.12, s32[16]{0:T(128)} %bitcast.13, bf16[128,3072]{1,0:T(8,128)(2,1)} %weight.1, bf16[1,3072]{1,0:T(2,128)(2,1)} %gate.1), custom_call_target="tpu_custom_call" | custom-call | flops 10000000000 | bytes 10000000 | tf_op jit(solution)/shard_map/attention_and_projection/pallas_call | solution.py:218
  82.0 1.4 %copy.9 = bf16[1,384,3072]{2,1,0:T(8,128)(2,1)} copy(bf16[1,384,3072]{2,1,0:T(8,128)(2,1)S(1)} %bitcast.8) | data formatting | bytes 4718592

commit v3 on v2

--- a/solution.py
+++ b/solution.py
@@ -20,28 +20,35 @@
 COMING = AWAY * PIECES + PIECES // 2
 EARLY = 7
 NCHUNK = 512
-LAST = 2
+QUERY_TURNS = (0, 1, 3, 4, 5, 6, 7, 8, 9, 2, 10, 14, 11, 12, 13)
 MESH = pl.DeviceIdType.MESH
 ORDER_X = (1, 3, 0, 0, 1, 3, 1, 3, 2, 2, 1, 3, 2, 2, 0, 0)
 ORDER_Y = (0, 0, 1, 3, 1, 3, 3, 1, 1, 3, 2, 2, 2, 0, 2, 0)
 TO_EXP2 = math.log2(math.e) / math.sqrt(HD)
 
 
-def packed(digits):
-    value = sum(d << (2 * i) for i, d in enumerate(digits))
-    return value - (1 << 32) if value >= 1 << 31 else value
+def packed(digits, bits):
+    value = sum(d << (bits * i) for i, d in enumerate(digits))
+    return jnp.int32(value - (1 << 32) if value >= 1 << 31 else value)
 
 
 def digit(digits, i):
     if isinstance(i, int):
         return digits[i]
-    return lax.shift_right_logical(jnp.int32(packed(digits)), 2 * i) & 3
-
-
-def turn(n):
-    if isinstance(n, int):
-        return LAST if n == PEERS - 1 else n + (n >= LAST)
-    return jnp.where(n == PEERS - 1, LAST, jnp.where(n < LAST, n, n + 1))
+    return lax.shift_right_logical(packed(digits, 2), 2 * i) & 3
+
+
+def entry(values, i):
+    if isinstance(i, int):
+        return values[i]
+    half = packed(values[:8], 4), packed(values[8:], 4)
+    return lax.shift_right_logical(jnp.where(i < 8, *half), 4 * (i % 8)) & 15
+
+
+TURNS = (PEERS, *QUERY_TURNS)
+TURN_X = tuple(ORDER_X[i] for i in TURNS)
+TURN_Y = tuple(ORDER_Y[i] for i in TURNS)
+PLACES = tuple(tuple(zip(TURN_X, TURN_Y)).index((d // SIDE, d % SIDE)) for d in range(SIDE * SIDE))
 
 
 def attend(query, kbuf, vbuf, key_tiles, tile_counts, a):
@@ -75,7 +82,7 @@
     query_rows, key_rows, value_rows, key_tiles, tile_counts, weight, gate, out,
     kbuf, vbuf, qbuf, obuf, orecv, wbuf, acc,
     k_send, k_recv, v_send, v_recv, q_send, q_recv, o_send, o_recv, own_sem,
-    w_send, w_recv, c_send, c_recv,
+    w_send, w_recv, c_send, c_recv, c_far, ready,
 ):
     seq, dp = lax.axis_index("seq"), lax.axis_index("dp")
     x, y, z, core = seq // SIDE, seq % SIDE, dp // 2, dp % 2
@@ -98,8 +105,12 @@
     barrier = pltpu.get_barrier_semaphore()
     for i in range(PEERS):
         pl.semaphore_signal(barrier, inc=1, device_id=(partner(i), dp), device_id_type=MESH)
-    for where in (*nexts, other):
-        pl.semaphore_signal(barrier, inc=1, device_id=(seq, where), device_id_type=MESH)
+    pl.semaphore_signal(barrier, inc=1, device_id=(seq, other), device_id_type=MESH)
+
+    @pl.when(z % 2 == 0)
+    def _():
+        for where in nexts:
+            pl.semaphore_signal(barrier, inc=1, device_id=(seq, where), device_id_type=MESH)
 
     def head_columns(i):
         return pl.ds(pl.multiple_of(partner(i) * HD, HD), HD)
@@ -113,7 +124,13 @@
     ]
     for copy in own:
         copy.start()
-    pl.semaphore_wait(barrier, PEERS + 3)
+    pl.semaphore_wait(barrier, PEERS + 1 + 2 * (z % 2))
+
+    @pl.when(z % 2 == 1)
+    def _():
+        for where in nexts:
+            pl.semaphore_signal(ready, inc=1, device_id=(seq, where), device_id_type=MESH)
+
 
     def piece(p):
         return pl.ds(pl.multiple_of(p * PIECE, PIECE), PIECE)
@@ -122,19 +139,23 @@
         place = wbuf.at[block, piece(p)]
         return remote(place if src is None else src, place, w_send, w_recv.at[way, n], (seq, nexts[way]))
 
+    for i in range(PEERS):
+        remote(key_rows.at[:, head_columns(i)], kbuf.at[seq], k_send, k_recv, (partner(i), dp)).start()
+    for i in range(PEERS):
+        remote(value_rows.at[:, head_columns(i)], vbuf.at[seq], v_send, v_recv, (partner(i), dp)).start()
+    for i in range(PEERS):
+        remote(query_rows.at[:, head_columns(i)], qbuf.at[i], q_send, q_recv.at[i], (partner(i), dp)).start()
+    remote(weight, wbuf.at[dp], c_send, c_recv, (seq, other)).start()
+
+    @pl.when(z % 2 == 0)
+    def _():
+        pl.semaphore_wait(ready, 2)
+
     for p in range(PIECES):
         for way in range(2):
             hop(way, p, p, dp, weight.at[piece(p)]).start()
 
-    for i in range(PEERS):
-        remote(key_rows.at[:, head_columns(i)], kbuf.at[seq], k_send, k_recv, (partner(i), dp)).start()
-    for i in range(PEERS):
-        remote(value_rows.at[:, head_columns(i)], vbuf.at[seq], v_send, v_recv, (partner(i), dp)).start()
-    for i in range(PEERS):
-        remote(query_rows.at[:, head_columns(i)], qbuf.at[i], q_send, q_recv.at[i], (partner(i), dp)).start()
-    remote(weight, wbuf.at[dp], c_send, c_recv, (seq, other)).start()
-
-    def tick(n):
+    def tick(n, swapped):
         q = n % PIECES
         for way in range(2):
             p = q + way * (PIECES // 2) * (n // (AWAY * PIECES))
@@ -148,27 +169,27 @@
                 hop(way, jnp.where(n < (AWAY - 1) * PIECES, n + PIECES, last), p, block).start()
 
             place = wbuf.at[block, piece(p)]
-            remote(place, place, c_send, c_recv, (seq, other)).start()
+            remote(place, place, c_send, swapped, (seq, other)).start()
 
     for n in range(EARLY):
-        tick(n)
+        tick(n, c_recv)
     bytes_of(kbuf, len(own) - 1 + HD * D // (TILE * HD), own_sem).wait()
     bytes_of(kbuf, PEERS, k_recv).wait()
     bytes_of(vbuf, PEERS, v_recv).wait()
 
-    orecv[PEERS] = attend(qbuf[PEERS], kbuf, vbuf, key_tiles, tile_counts, seq)
+    orecv[seq] = attend(qbuf[PEERS], kbuf, vbuf, key_tiles, tile_counts, seq)
 
     def answer(i):
         a = partner(i, -1)
-        return remote(obuf.at[i], orecv.at[i], o_send, o_recv.at[i], (a, dp))
+        return remote(obuf.at[i], orecv.at[seq], o_send, o_recv.at[seq], (a, dp))
 
     def step(n, carry):
-        i = turn(n)
+        i = entry(QUERY_TURNS, n)
         a = partner(i, -1)
 
         @pl.when(n % 3 == 1)
         def _():
-            tick(EARLY + n // 3)
+            tick(EARLY + n // 3, c_recv)
 
         pltpu.make_async_copy(qbuf.at[i], qbuf.at[i], q_recv.at[i]).wait()
         obuf[i] = attend(qbuf[i], kbuf, vbuf, key_tiles, tile_counts, a)
@@ -176,29 +197,44 @@
         return carry
 
     lax.fori_loop(0, PEERS, step, 0)
-    for n in range(EARLY + PEERS // 3, COMING):
-        tick(n)
-    bytes_of(wbuf, RING, c_recv).wait()
-
-    order = [PEERS, *(turn(n) for n in range(PEERS))]
-    done = 0
-    for group in (4, 4, 4, 2, 2):
-        these = order[done : done + group]
-        done += group
-        for i in these:
-            if i < PEERS:
-                pltpu.make_async_copy(orecv.at[i], orecv.at[i], o_recv.at[i]).wait()
-        rows = jnp.concatenate([orecv[i] for i in these], axis=1)
+    far = (z + RING // 2) % RING * 2
+    at_a = entry(PLACES, (far // SIDE - x + SIDE) % SIDE * SIDE + (far % SIDE - y + SIDE) % SIDE)
+    at_b = entry(PLACES, ((far + 1) // SIDE - x + SIDE) % SIDE * SIDE + ((far + 1) % SIDE - y + SIDE) % SIDE)
+    low, high = jnp.minimum(at_a, at_b), jnp.maximum(at_a, at_b)
+
+    def near_head(k):
+        k = k + jnp.where(k >= low, 1, 0)
+        k = k + jnp.where(k >= high, 1, 0)
+        return (x + digit(TURN_X, k)) % SIDE * SIDE + (y + digit(TURN_Y, k)) % SIDE
+
+    def project(heads, first=False, last=False):
+        for h in heads:
+
+            @pl.when(h != seq)
+            def _():
+                pltpu.make_async_copy(orecv.at[h], orecv.at[h], o_recv.at[h]).wait()
+
+        rows = jnp.concatenate([orecv[h] for h in heads], axis=1)
         for n in range(0, D, NCHUNK):
             at = pl.ds(n, NCHUNK)
-            block = jnp.concatenate([wbuf[partner(i), :, at] for i in these], axis=0)
+            block = jnp.concatenate([wbuf[h, :, at] for h in heads], axis=0)
             product = jnp.dot(rows, block, preferred_element_type=jnp.float32)
-            if done > group:
+            if not first:
                 product = acc[:, at] + product
-            if done <= PEERS:
+            if last:
+                out[:, at] = (gate[:, at].astype(jnp.float32) * product).astype(jnp.bfloat16)
+            else:
                 acc[:, at] = product
-            else:
-                out[:, at] = (gate[:, at].astype(jnp.float32) * product).astype(jnp.bfloat16)
+
+    bytes_of(wbuf, RING - 1, c_recv).wait()
+    project([near_head(k) for k in range(4)], first=True)
+    tick(COMING - 2, c_far)
+    tick(COMING - 1, c_far)
+    project([near_head(k) for k in range(4, 8)])
+    bytes_of(wbuf, 1, c_far).wait()
+    project([far, far + 1])
+    project([near_head(k) for k in range(8, 12)])
+    project([near_head(k) for k in range(12, 14)], last=True)
 
     bytes_of(kbuf, PEERS, k_send).wait()
     bytes_of(vbuf, PEERS, v_send).wait()
@@ -229,8 +265,8 @@
             pltpu.VMEM((tiles, TILE, HD), jnp.bfloat16),
             pltpu.VMEM((blocks, HD, D), jnp.bfloat16),
             pltpu.VMEM((TILE, D), jnp.float32),
-            dma, dma, dma, dma, dma, dma((PEERS,)), dma, dma((PEERS,)), dma,
-            dma, dma((2, COMING)), dma, dma,
+            dma, dma, dma, dma, dma, dma((PEERS,)), dma, dma((tiles,)), dma,
+            dma, dma((2, COMING)), dma, dma, dma, pltpu.SemaphoreType.REGULAR,
         ],
         compiler_params=pltpu.CompilerParams(
             collective_id=0, has_side_effects=True, vmem_limit_bytes=60 << 20

time: 83.5 us -> 81.4 us (0.975)
  Pallas kernels: 82 us -> 79.5 us
    pallas_call x1, Pallas kernels: 82 us -> 79.5 us  [shards(): pl.pallas_call(kernel, name='attention_and_projection', out_shape=pltpu.V...]
where the time goes in v3:
time: 81.4 us; the launch traced here: 80.9 us
  Pallas kernels  79.5 us (98%)
  local copies, waits for them, and re-layouts  1.41 us (2%)
    pallas_call x1, Pallas kernels, shards(): pl.pallas_call(kernel, name='attention_and_projection', out_shape=pltpu.V...  79.5 us

profile of v3, /device:TPU:1, one launch (start us, length us, event | category | flops | bytes accessed | tf_op | source)
XLA Modules:
  0.0 80.9 jit_solution(5559856062948295201)
XLA Ops:
  0.0 79.5 %attention_and_projection.1 = bf16[384,3072]{1,0:T(8,128)(2,1)S(1)} custom-call(bf16[384,2048]{1,0:T(8,128)(2,1)} %bitcast.9, bf16[384,2048]{1,0:T(8,128)(2,1)} %bitcast.10, bf16[384,2048]{1,0:T(8,128)(2,1)} %bitcast.11, s32[4,16]{1,0:T(4,128)} %bitcast.12, s32[16]{0:T(128)} %bitcast.13, bf16[128,3072]{1,0:T(8,128)(2,1)} %weight.1, bf16[1,3072]{1,0:T(2,128)(2,1)} %gate.1), custom_call_target="tpu_custom_call" | custom-call | flops 10000000000 | bytes 10000000 | tf_op jit(solution)/shard_map/attention_and_projection/pallas_call | solution.py:254
  79.5 1.4 %copy.9 = bf16[1,384,3072]{2,1,0:T(8,128)(2,1)} copy(bf16[1,384,3072]{2,1,0:T(8,128)(2,1)S(1)} %bitcast.8) | data formatting | bytes 4718592

commit v4 on v3

--- a/solution.py
+++ b/solution.py
@@ -79,9 +79,9 @@
 
 
 def kernel(
-    query_rows, key_rows, value_rows, key_tiles, tile_counts, weight, gate, out,
-    kbuf, vbuf, qbuf, obuf, orecv, wbuf, acc,
-    k_send, k_recv, v_send, v_recv, q_send, q_recv, o_send, o_recv, own_sem,
+    query_rows, key_rows, value_rows, key_tiles_far, tile_counts_far, weight, gate_far, out,
+    key_tiles, tile_counts, gate, kbuf, vbuf, qbuf, obuf, orecv, wbuf, acc,
+    k_send, k_recv, v_send, v_recv, q_send, q_recv, o_send, o_recv, own_sem, list_sem,
     w_send, w_recv, c_send, c_recv, c_far, ready,
 ):
     seq, dp = lax.axis_index("seq"), lax.axis_index("dp")
@@ -122,7 +122,12 @@
         pltpu.make_async_copy(query_rows.at[:, mine], qbuf.at[PEERS], own_sem),
         pltpu.make_async_copy(weight, wbuf.at[dp], own_sem),
     ]
-    for copy in own:
+    lists = [
+        pltpu.make_async_copy(key_tiles_far, key_tiles, list_sem.at[0]),
+        pltpu.make_async_copy(tile_counts_far, tile_counts, list_sem.at[1]),
+        pltpu.make_async_copy(gate_far, gate, list_sem.at[2]),
+    ]
+    for copy in (*own, *lists):
         copy.start()
     pl.semaphore_wait(barrier, PEERS + 1 + 2 * (z % 2))
 
@@ -174,6 +179,8 @@
     for n in range(EARLY):
         tick(n, c_recv)
     bytes_of(kbuf, len(own) - 1 + HD * D // (TILE * HD), own_sem).wait()
+    for copy in lists:
+        copy.wait()
     bytes_of(kbuf, PEERS, k_recv).wait()
     bytes_of(vbuf, PEERS, v_recv).wait()
 
@@ -248,16 +255,18 @@
     dma = pltpu.SemaphoreType.DMA
     far = pl.BlockSpec(memory_space=pltpu.HBM)
     near = pl.BlockSpec(memory_space=pltpu.VMEM)
-    scalars = pl.BlockSpec(memory_space=pltpu.SMEM)
     tiles = PEERS + 1
     blocks = RING * 2
     result = pl.pallas_call(
         kernel,
         name="attention_and_projection",
         out_shape=pltpu.VMEM((TILE, D), jnp.bfloat16),
-        in_specs=[far, far, far, scalars, scalars, far, near],
+        in_specs=[far] * 7,
         out_specs=near,
         scratch_shapes=[
+            pltpu.SMEM((MAXK, tiles), jnp.int32),
+            pltpu.SMEM((tiles,), jnp.int32),
+            pltpu.VMEM((1, D), jnp.bfloat16),
             pltpu.VMEM((tiles, TILE, HD), jnp.bfloat16),
             pltpu.VMEM((tiles, TILE, HD), jnp.bfloat16),
             pltpu.VMEM((tiles, TILE, HD), jnp.bfloat16),
@@ -265,7 +274,7 @@
             pltpu.VMEM((tiles, TILE, HD), jnp.bfloat16),
             pltpu.VMEM((blocks, HD, D), jnp.bfloat16),
             pltpu.VMEM((TILE, D), jnp.float32),
-            dma, dma, dma, dma, dma, dma((PEERS,)), dma, dma((tiles,)), dma,
+            dma, dma, dma, dma, dma, dma((PEERS,)), dma, dma((tiles,)), dma, dma((3,)),
             dma, dma((2, COMING)), dma, dma, dma, pltpu.SemaphoreType.REGULAR,
         ],
         compiler_params=pltpu.CompilerParams(

time: 81.4 us -> 80.7 us (level)
  no operation moved by 1% of the time
where the time goes in v4:
time: 80.7 us; the launch traced here: 80.2 us
  Pallas kernels  78.8 us (98%)
  local copies, waits for them, and re-layouts  1.41 us (2%)
    pallas_call x1, Pallas kernels, shards(): pl.pallas_call(kernel, name='attention_and_projection', out_shape=pltpu.V...  78.8 us

profile of v4, /device:TPU:1, one launch (start us, length us, event | category | flops | bytes accessed | tf_op | source)
XLA Modules:
  0.0 80.2 jit_solution(8628054725206180576)
XLA Ops:
  0.0 78.8 %attention_and_projection.1 = bf16[384,3072]{1,0:T(8,128)(2,1)S(1)} custom-call(bf16[384,2048]{1,0:T(8,128)(2,1)} %bitcast.9, bf16[384,2048]{1,0:T(8,128)(2,1)} %bitcast.10, bf16[384,2048]{1,0:T(8,128)(2,1)} %bitcast.11, s32[4,16]{1,0:T(4,128)} %bitcast.12, s32[16]{0:T(128)} %bitcast.13, bf16[128,3072]{1,0:T(8,128)(2,1)} %weight.1, bf16[1,3072]{1,0:T(2,128)(2,1)} %gate_far.1), custom_call_target="tpu_custom_call" | custom-call | flops 10000000000 | bytes 10000000 | tf_op jit(solution)/shard_map/attention_and_projection/pallas_call | solution.py:260
  78.8 1.4 %copy.9 = bf16[1,384,3072]{2,1,0:T(8,128)(2,1)} copy(bf16[1,384,3072]{2,1,0:T(8,128)(2,1)S(1)} %bitcast.8) | data formatting | bytes 4718592
